TPU v7x, 128 devices: a whole 4x4x4 slice. The times are simulated.
128 devices in a mesh: seq: 32 (over x, y, core), chan: 4 (over z).
Axes of the slice: x: 4, y: 4, z: 4, core: 2. Of those that a mesh axis runs over, the one named last changes fastest.
Arguments:
- tokens: bfloat16 [16384, 8192], P('seq', 'chan'), may hold values from -6 to 6
- w_in: bfloat16 [8192, 4096], P('chan'), may hold values from -0.0625 to 0.0625
- gate_k: bfloat16 [16384, 4096], P('seq', 'chan'), may hold values from -6 to 6
- gate_q: bfloat16 [16384, 4096], P('seq', 'chan'), may hold values from -6 to 6
- filters: bfloat16 [16384, 4096], P('seq', 'chan')
- skip: float32 [4096], P('chan'), may hold values from 0.3 to 1.5
Outputs:
- gated: bfloat16 [16384, 4096], P('seq', 'chan')
All inputs are finite; a program needn't handle non-finite values.
Results may differ from a plain program's by a relative error of at most 0.009.
Values may be sent and summed in bfloat16 or wider, within the bound.
A program may use at most 192 MiB of HBM per device.

v0:
```python
import math

import jax
import jax.numpy as jnp
from jax import lax
from jax.sharding import PartitionSpec as P

highest = lax.Precision.HIGHEST


def phase_table(first, second, modulus):
    product = first[:, None] * second[None, :] % modulus
    angle = product.astype(jnp.float32) * (2.0 * math.pi / modulus)
    return (jnp.cos(angle), jnp.sin(angle))


def slot_order(seq_count):
    row_index = jnp.arange(2 * seq_count, dtype=jnp.int32)
    column = row_index // 2
    second = jnp.where(column == 0, seq_count, 2 * seq_count - column)
    return jnp.where(row_index % 2 == 0, column, second)


def complex_product(form, left_re, left_im, right_re, right_im):
    real = jnp.einsum(form, left_re, right_re, precision=highest) - jnp.einsum(
        form, left_im, right_im, precision=highest
    )
    imag = jnp.einsum(form, left_re, right_im, precision=highest) + jnp.einsum(
        form, left_im, right_re, precision=highest
    )
    return (real, imag)


def local(tokens, w_in, gate_k, gate_q, filters, skip):
    seq_count = lax.axis_size("seq")
    seq_index = lax.axis_index("seq")
    block_rows = tokens.shape[0]
    piece_rows = block_rows // seq_count
    chan_width = gate_k.shape[1]
    span_len = 2 * seq_count
    full_len = span_len * block_rows
    terms = jnp.dot(tokens, w_in, preferred_element_type=jnp.float32)
    value = lax.psum_scatter(terms, "chan", scatter_dimension=1, tiled=True)
    mixed = (gate_k.astype(jnp.float32) * value).astype(jnp.bfloat16)
    stacked = jnp.stack([mixed, filters]).reshape(2, seq_count, piece_rows, chan_width)
    columns = lax.all_to_all(stacked, "seq", split_axis=1, concat_axis=1, tiled=True).astype(
        jnp.float32
    )
    order = slot_order(seq_count)
    cos_a, sin_a = phase_table(order, jnp.arange(seq_count, dtype=jnp.int32), span_len)
    local_pos = seq_index * piece_rows + jnp.arange(piece_rows, dtype=jnp.int32)
    cos_t, sin_t = phase_table(order, local_pos, full_len)
    twid_re = cos_t[:, :, None]
    twid_im = -sin_t[:, :, None]
    steps_b = jnp.arange(block_rows, dtype=jnp.int32)
    cos_b, sin_b = phase_table(steps_b, steps_b, block_rows)
    real = jnp.einsum("ra,sapc->srpc", cos_a, columns, precision=highest)
    imag = jnp.einsum("ra,sapc->srpc", -sin_a, columns, precision=highest)
    real, imag = (real * twid_re - imag * twid_im, real * twid_im + imag * twid_re)
    packed = jnp.stack([real, imag], 1).reshape(2, 2, seq_count, 2, piece_rows, chan_width)
    spectra = lax.all_to_all(
        packed.astype(jnp.bfloat16), "seq", split_axis=2, concat_axis=4, tiled=True
    ).astype(packed.dtype)[:, :, 0]
    spec_re, spec_im = complex_product(
        "kb,...bc->...kc", cos_b, -sin_b, spectra[:, 0], spectra[:, 1]
    )
    value_re, value_im = (spec_re[0], spec_im[0])
    filt_re, filt_im = (spec_re[1], spec_im[1])
    prod_re = value_re * filt_re - value_im * filt_im
    prod_im = value_re * filt_im + value_im * filt_re
    back_re, back_im = complex_product("bk,skc->sbc", cos_b, sin_b, prod_re, prod_im)
    own_freq = lax.dynamic_slice_in_dim(order, 2 * seq_index, 2)
    cos_i, sin_i = phase_table(own_freq, steps_b, full_len)
    inv_re = cos_i[:, :, None]
    inv_im = sin_i[:, :, None]
    turned_re = back_re * inv_re - back_im * inv_im
    turned_im = back_re * inv_im + back_im * inv_re
    outgoing = jnp.stack([turned_re, turned_im]).reshape(2, 2, seq_count, piece_rows, chan_width)
    incoming = lax.all_to_all(outgoing, "seq", split_axis=2, concat_axis=1, tiled=True)[:, :, 0]
    conv_rows = jnp.einsum("ra,rpc->apc", cos_a, incoming[0], precision=highest)
    conv_rows = conv_rows - jnp.einsum("ra,rpc->apc", sin_a, incoming[1], precision=highest)
    conv_rows = conv_rows * (1.0 / full_len)
    conv = lax.all_to_all(conv_rows, "seq", split_axis=0, concat_axis=1, tiled=True)[0]
    result = gate_q.astype(jnp.float32) * (conv + skip[None, :] * mixed.astype(jnp.float32))
    return result.astype(jnp.bfloat16)


def solution(mesh):
    in_specs = (
        P("seq", "chan"),
        P("chan", None),
        P("seq", "chan"),
        P("seq", "chan"),
        P("seq", "chan"),
        P("chan"),
    )
    out_specs = P("seq", "chan")
    return jax.shard_map(local, mesh=mesh, in_specs=in_specs, out_specs=out_specs, check_vma=False)
```

profile of v0, /device:TPU:1, one launch (start us, length us, event | category | flops | bytes accessed | tf_op | source)
XLA Modules:
  0.0 606.3 jit_solution(6732860649360592845)
XLA Ops:
  6.5 0.0 copy-start
  6.5 0.0 reduce-scatter.2.cloned.1.call-start
  6.5 1.6 copy-done
  8.1 14.4 %fusion.135 = f32[512,4096]{1,0:T(8,128)} fusion(bf16[512,2048]{1,0:T(8,128)(2,1)S(1)} %copy-done, bf16[2048,4096]{1,0:T(8,128)(2,1)} %param.7), kind=kOutput, calls=%fused_computation.158 | convolution fusion | flops 8589934592 | bytes 27262976 | tf_op jit(solution)/shard_map/dot_general | solution.py:42
  22.6 0.0 copy-start.6
  22.6 0.0 reduce-scatter.2.cloned.1.call-update
  22.6 0.0 copy-start.7
  22.6 84.1 %reduce-scatter.2.cloned.1.call-done = f32[512,1024]{1,0:T(8,128)} async-done(((f32[512,4096]{1,0:T(8,128)}), f32[512,1024]{1,0:T(8,128)}) %reduce-scatter.2.cloned.1.call-update) | async-done | bytes 2097168 | tf_op jit(solution)/shard_map/reduce_scatter | solution.py:43
  106.7 0.0 copy-done.6
  106.7 1.9 multiply_convert_fusion
  108.7 0.0 copy-start.4
  108.7 0.0 copy-done.7
  108.7 0.2 pad_maximum_fusion.2
  108.9 1.5 copy.29
  110.4 0.0 copy-done.4
  110.4 7.8 %all-to-all-start = ((bf16[2,32,16,1024]{3,2,0,1:T(8,128)(2,1)}), bf16[2,32,16,1024]{3,2,0,1:T(8,128)(2,1)S(1)}, u32[]{:S(2)}, u32[]{:S(2)}) async-start(bf16[2,32,16,1024]{3,2,0,1:T(8,128)(2,1)} %copy.29), calls=%async_computation.1 | async-start | bytes 4194304 | tf_op jit(solution)/shard_map/all_to_all | solution.py:46
  118.2 0.1 fusion.83
  118.4 28.0 %all-to-all-done = bf16[2,32,16,1024]{3,2,0,1:T(8,128)(2,1)S(1)} async-done(((bf16[2,32,16,1024]{3,2,0,1:T(8,128)(2,1)}), bf16[2,32,16,1024]{3,2,0,1:T(8,128)(2,1)S(1)}, u32[]{:S(2)}, u32[]{:S(2)}) %all-to-all-start) | async-done | bytes 2097184 | tf_op jit(solution)/shard_map/all_to_all | solution.py:46
  146.4 5.8 fusion.30
  152.2 12.3 %fusion.1 = (bf16[2,64,16,1024]{3,1,2,0:T(8,128)(2,1)}, bf16[2,64,16,1024]{3,1,2,0:T(8,128)(2,1)}) fusion(f32[2,16,1024,64]{2,3,1,0:T(8,128)S(1)} %fusion.30, f32[64,16]{0,1:T(8,128)S(1)} %get-tuple-element.14, f32[64,16]{0,1:T(8,128)S(1)} %get-tuple-element.13, s32[64]{0:T(128)S(1)} %compare_select_fusion.3, bf16[2,32,16,1024]{3,2,0,1:T(8,128)(2,1)S(1)} %all-to-all-done), kind=kOutput, calls=%fused_computation.5 | convolution fusion | flops 822114304 | bytes 18882816 | tf_op jit(solution)/shard_map/ra,sapc->srpc/dot_general | solution.py:58
  164.5 7.6 %stack.30 = bf16[2,1,32,2,16,1024]{5,3,2,4,0,1:T(2,128)(2,1)} reshape(bf16[2,64,16,1024]{3,1,2,0:T(8,128)(2,1)} %get-tuple-element.5) | data formatting | bytes 8388608 | tf_op jit(solution)/shard_map/stack | solution.py:60
  172.1 8.6 %copy.32 = bf16[2,1,32,2,16,1024]{5,4,3,1,0,2:T(8,128)(2,1)} copy(bf16[2,1,32,2,16,1024]{5,3,2,4,0,1:T(2,128)(2,1)} %stack.30) | data formatting | bytes 8388608 | tf_op jit(solution)/shard_map/stack | solution.py:60
  180.7 7.2 %stack.31 = bf16[2,1,32,2,16,1024]{5,3,2,4,0,1:T(2,128)(2,1)} reshape(bf16[2,64,16,1024]{3,1,2,0:T(8,128)(2,1)} %get-tuple-element.6) | data formatting | bytes 8388608 | tf_op jit(solution)/shard_map/stack | solution.py:60
  187.9 0.0 copy-start.3
  187.9 8.7 %copy.33 = bf16[2,1,32,2,16,1024]{5,4,3,1,0,2:T(8,128)(2,1)} copy(bf16[2,1,32,2,16,1024]{5,3,2,4,0,1:T(2,128)(2,1)} %stack.31) | data formatting | bytes 8388608 | tf_op jit(solution)/shard_map/stack | solution.py:60
  196.7 0.0 copy-done.3
  196.7 6.2 %pad_maximum_fusion = bf16[2,2,32,2,16,1024]{5,4,3,1,0,2:T(8,128)(2,1)} fusion(bf16[2,1,32,2,16,1024]{5,4,3,1,0,2:T(8,128)(2,1)} %copy.33, bf16[2,1,32,2,16,1024]{5,4,3,1,0,2:T(8,128)(2,1)S(1)} %copy-done.3), kind=kLoop, calls=%fused_computation | loop fusion | flops 4194304 | bytes 16777216 | tf_op jit(solution)/shard_map/stack | solution.py:60
  202.9 5.6 all-to-all-start.1
  208.5 0.1 dynamic_slice.3
  208.6 0.2 fusion.85
  208.8 106.4 %all-to-all-done.1 = bf16[2,2,32,2,16,1024]{5,4,3,1,0,2:T(8,128)(2,1)} async-done(((bf16[2,2,32,2,16,1024]{5,4,3,1,0,2:T(8,128)(2,1)}), bf16[2,2,32,2,16,1024]{5,4,3,1,0,2:T(8,128)(2,1)}, u32[]{:S(2)}, u32[]{:S(2)}) %all-to-all-start.1) | async-done | bytes 8388640 | tf_op jit(solution)/shard_map/all_to_all | solution.py:61
  315.1 8.5 %copy.34 = bf16[2,2,32,2,16,1024]{5,4,2,3,1,0:T(8,128)(2,1)} copy(bf16[2,2,32,2,16,1024]{5,4,3,1,0,2:T(8,128)(2,1)} %all-to-all-done.1) | data formatting | bytes 16777216 | tf_op jit(solution)/shard_map/all_to_all | solution.py:61
  323.7 0.0 copy-start.2
  323.7 14.7 %fusion.17 = f32[2,2,1024,512]{3,2,1,0:T(8,128)S(1)} fusion(bf16[2,2,2,512,1024]{4,3,2,1,0:T(8,128)(2,1)} %bitcast.132), kind=kOutput, calls=%fused_computation.31 | convolution fusion | flops 12888571904 | bytes 12582912 | tf_op jit(solution)/shard_map/kb,...bc->...kc/dot_general | solution.py:25
  338.3 0.0 copy-done.2
  338.3 15.6 %fusion.16 = f32[2,2,1024,512]{3,2,1,0:T(8,128)} fusion(bf16[2,2,2,512,1024]{4,3,2,1,0:T(8,128)(2,1)S(1)} %bitcast.133), kind=kOutput, calls=%fused_computation.30 | convolution fusion | flops 12888834048 | bytes 12582912 | tf_op jit(solution)/shard_map/kb,...bc->...kc/dot_general | solution.py:28
  354.0 12.5 %subtract_bitcast_fusion = f32[2,2,512,1024]{2,3,1,0:T(8,128)S(1)} fusion(f32[2,2,1024,512]{3,2,1,0:T(8,128)S(1)} %fusion.17, bf16[2,2,2,512,1024]{4,3,2,1,0:T(8,128)(2,1)S(1)} %bitcast.134), kind=kOutput, calls=%fused_computation.11 | convolution fusion | flops 12890931200 | bytes 20971520 | tf_op jit(solution)/shard_map/kb,...bc->...kc/dot_general | solution.py:25
  366.5 16.8 %add_bitcast_fusion = f32[2,2,512,1024]{2,3,1,0:T(8,128)S(1)} fusion(f32[2,2,1024,512]{3,2,1,0:T(8,128)} %fusion.16, bf16[2,2,2,512,1024]{4,3,2,1,0:T(8,128)(2,1)S(1)} %bitcast.135), kind=kOutput, calls=%fused_computation.10 | convolution fusion | flops 12890669056 | bytes 20971520 | tf_op jit(solution)/shard_map/kb,...bc->...kc/dot_general | solution.py:28
  383.4 2.3 multiply_subtract_fusion.1
  385.7 10.7 %fusion.10 = f32[2,1024,512]{1,2,0:T(8,128)S(1)} fusion(f32[1,2,512,1024]{2,3,1,0:T(8,128)S(1)} %get-tuple-element.8), kind=kOutput, calls=%fused_computation.20 | convolution fusion | flops 6446120960 | bytes 8388608 | tf_op jit(solution)/shard_map/bk,skc->sbc/dot_general | solution.py:25
  396.4 11.3 %fusion.8 = f32[2,1024,512]{1,2,0:T(8,128)S(1)} fusion(f32[1,2,512,1024]{2,3,1,0:T(8,128)S(1)} %get-tuple-element.8), kind=kOutput, calls=%fused_computation.18 | convolution fusion | flops 6446120960 | bytes 8388608 | tf_op jit(solution)/shard_map/bk,skc->sbc/dot_general | solution.py:28
  407.7 11.2 %fusion.20 = f32[2,1024,512]{1,2,0:T(8,128)S(1)} fusion(f32[2,1024,512]{1,2,0:T(8,128)S(1)} %fusion.10, f32[1,2,512,1024]{2,3,1,0:T(8,128)S(1)} %get-tuple-element.7), kind=kOutput, calls=%fused_computation.34 | convolution fusion | flops 6447169536 | bytes 12582912 | tf_op jit(solution)/shard_map/bk,skc->sbc/dot_general | solution.py:25
  419.0 12.0 %multiply_subtract_fusion = (f32[2,1024,512]{1,2,0:T(8,128)S(1)}, f32[2,1024,512]{1,2,0:T(8,128)S(1)}) fusion(f32[2,1024,512]{1,2,0:T(8,128)S(1)} %fusion.20, f32[2,512]{1,0:T(2,128)S(1)} %get-tuple-element.16, f32[2,512]{1,0:T(2,128)S(1)} %get-tuple-element.15, f32[2,1024,512]{1,2,0:T(8,128)S(1)} %fusion.8, f32[1,2,512,1024]{2,3,1,0:T(8,128)S(1)} %get-tuple-element.7), kind=kOutput, calls=%fused_computation.27 | convolution fusion | flops 6453460992 | bytes 20979712 | tf_op jit(solution)/shard_map/bk,skc->sbc/dot_general | solution.py:28
  431.0 1.7 pad_maximum_fusion.1
  432.6 1.7 copy.54
  434.3 119.1 %all_to_all.44 = f32[2,2,32,16,1024]{4,3,1,0,2:T(8,128)S(1)} all-to-all(f32[2,2,32,16,1024]{4,3,1,0,2:T(8,128)S(1)} %copy.54), channel_id=1, replica_groups=mesh['seq'=32,'chan'=4] {'seq'}, dimensions={2} | all-to-all | bytes 16777216 | tf_op jit(solution)/shard_map/all_to_all | solution.py:79
  553.5 1.7 fusion.134
  555.1 4.5 fusion.4
  559.7 4.7 subtract_multiply_fusion
  564.3 0.0 copy-start.5
  564.3 0.0 copy-start.8
  564.4 0.0 copy-start.9
  564.4 0.0 copy-start.1
  564.4 1.2 copy.45
  565.6 31.9 %all_to_all.45 = f32[32,16,1024]{2,1,0:T(8,128)S(1)} all-to-all(f32[32,16,1024]{2,1,0:T(8,128)S(1)} %copy.45), channel_id=1, replica_groups=mesh['seq'=32,'chan'=4] {'seq'}, dimensions={0} | all-to-all | bytes 4194304 | tf_op jit(solution)/shard_map/all_to_all | solution.py:83
  597.5 0.0 copy-done.5
  597.5 0.0 copy-done.8
  597.5 0.0 copy-done.9
  597.5 1.5 fusion.27
  599.0 0.0 copy-done.1
  (2 shorter events, 0.0 us)
Async XLA Ops:
  6.5 1.6 copy-start
  6.5 100.2 %reduce-scatter.2.cloned.1.call-start = ((), (), s32[]{:S(2)}) async-start(), calls=%async_computation.5 | async-start | bytes 10485760 | tf_op jit(solution)/shard_map/reduce_scatter | solution.py:43
  22.6 84.2 %copy-start.6 = (bf16[512,1024]{1,0:T(8,128)(2,1)S(1)}, bf16[512,1024]{1,0:T(8,128)(2,1)}, u32[]{:S(2)}) copy-start(bf16[512,1024]{1,0:T(8,128)(2,1)} %param.8) | copy-start | bytes 3145732
  22.6 86.1 %copy-start.7 = (bf16[512,1024]{1,0:T(8,128)(2,1)S(1)}, bf16[512,1024]{1,0:T(8,128)(2,1)}, u32[]{:S(2)}) copy-start(bf16[512,1024]{1,0:T(8,128)(2,1)} %param.10) | copy-start | bytes 3145732
  108.7 1.7 copy-start.4
  110.4 36.0 %all-to-all-start = ((bf16[2,32,16,1024]{3,2,0,1:T(8,128)(2,1)}), bf16[2,32,16,1024]{3,2,0,1:T(8,128)(2,1)S(1)}, u32[]{:S(2)}, u32[]{:S(2)}) async-start(bf16[2,32,16,1024]{3,2,0,1:T(8,128)(2,1)} %copy.29), calls=%async_computation.1 | async-start | bytes 4194304 | tf_op jit(solution)/shard_map/all_to_all | solution.py:46
  187.9 8.7 %copy-start.3 = (bf16[2,1,32,2,16,1024]{5,4,3,1,0,2:T(8,128)(2,1)S(1)}, bf16[2,1,32,2,16,1024]{5,4,3,1,0,2:T(8,128)(2,1)}, u32[]{:S(2)}) copy-start(bf16[2,1,32,2,16,1024]{5,4,3,1,0,2:T(8,128)(2,1)} %copy.32) | copy-start | bytes 12582916
  202.9 112.2 %all-to-all-start.1 = ((bf16[2,2,32,2,16,1024]{5,4,3,1,0,2:T(8,128)(2,1)}), bf16[2,2,32,2,16,1024]{5,4,3,1,0,2:T(8,128)(2,1)}, u32[]{:S(2)}, u32[]{:S(2)}) async-start(bf16[2,2,32,2,16,1024]{5,4,3,1,0,2:T(8,128)(2,1)} %pad_maximum_fusion), calls=%async_computation.2 | async-start | bytes 16777216 | tf_op jit(solution)/shard_map/all_to_all | solution.py:61
  323.7 14.7 %copy-start.2 = (bf16[2,2,32,2,16,1024]{5,4,2,3,1,0:T(8,128)(2,1)S(1)}, bf16[2,2,32,2,16,1024]{5,4,2,3,1,0:T(8,128)(2,1)}, u32[]{:S(2)}) copy-start(bf16[2,2,32,2,16,1024]{5,4,2,3,1,0:T(8,128)(2,1)} %copy.34) | copy-start | bytes 25165828
  564.3 33.1 %copy-start.5 = (bf16[512,1024]{1,0:T(8,128)(2,1)S(1)}, bf16[512,1024]{1,0:T(8,128)(2,1)}, u32[]{:S(2)}) copy-start(bf16[512,1024]{1,0:T(8,128)(2,1)} %copy-done.4) | copy-start | bytes 3145732
  564.3 33.1 %copy-start.8 = (bf16[512,1024]{1,0:T(8,128)(2,1)S(1)}, bf16[512,1024]{1,0:T(8,128)(2,1)}, u32[]{:S(2)}) copy-start(bf16[512,1024]{1,0:T(8,128)(2,1)} %param.9) | copy-start | bytes 3145732
  564.4 33.1 %copy-start.9 = (f32[1024]{0:T(1024)S(1)}, f32[1024]{0:T(1024)}, u32[]{:S(2)}) copy-start(f32[1024]{0:T(1024)} %param.11) | copy-start | bytes 12292
  564.4 34.7 %copy-start.1 = (bf16[512,2048]{1,0:T(8,128)(2,1)S(1)}, bf16[512,2048]{1,0:T(8,128)(2,1)}, u32[]{:S(2)}) copy-start(bf16[512,2048]{1,0:T(8,128)(2,1)} %param.6) | copy-start | bytes 6291460
Sparse Core Ops, SparseCore 0:
  22.7 83.9 reduce-scatter.1
where the time goes:
time: 611 us; the launch traced here: 606 us
  waiting for transfers between devices  219 us (36%)
  blocking collectives  151 us (25%)
  matrix products  147 us (24%)
  local copies, waits for them, and re-layouts  48.4 us (8%)
  other arithmetic  14.2 us (2%)
  between operations  14.1 us (2%)
  starting transfers between devices  13.4 us (2%)
    all_to_all x1, blocking collectives, local(): lax.all_to_all(outgoing, 'seq', split_axis=2, concat_axis=1, tiled=True)  119 us
    all_to_all x1, waiting for transfers between devices, local(): lax.all_to_all(packed.astype(jnp.bfloat16), 'seq', split_axis=2, concat_a...  106 us
    reduce_scatter x1, waiting for transfers between devices, local(): value = lax.psum_scatter(terms, 'chan', scatter_dimension=1, tiled=True)  84.1 us
    another operation x4, local copies, waits for them, and re-layouts, local(): jnp.stack([real, imag], 1)  32.1 us
    all_to_all x1, blocking collectives, local(): lax.all_to_all(conv_rows, 'seq', split_axis=0, concat_axis=1, tiled=True)[0]  31.9 us
    dot_general x2, matrix products, complex_product(): jnp.einsum(form, left_re, right_im, precision=highest)  28.2 us
    all_to_all x1, waiting for transfers between devices, local(): lax.all_to_all(stacked, 'seq', split_axis=1, concat_axis=1, tiled=True)  28 us
    dot_general x2, matrix products, complex_product(): jnp.einsum(form, left_im, right_re, precision=highest)  27.6 us
  transfers between devices with their start and end apart: 3, of which 3 were waited for; matrix products, arithmetic and copies ran while one was open for 0% of the time, Pallas kernels for 0%

commit v1 on v0

v1 whole, which is shorter than its diff:
```python
import math

import jax
import jax.numpy as jnp
import numpy as np
from jax import lax
from jax.experimental import pallas as pl
from jax.experimental.pallas import tpu as pltpu
from jax.sharding import PartitionSpec as P

MESH = pl.DeviceIdType.MESH
SEQ = 32
CHAN = 4
ROWS = 512
FEAT = 2048
WIDTH = 1024
N1 = 128
OWN_A = ROWS // N1
NC = 4
CW = WIDTH // NC
CD = CW // SEQ
BR = OWN_A * CD
HALF = ROWS // 2
F32, BF16 = jnp.float32, jnp.bfloat16


def tables():
    n = N1 * N1
    k = np.arange(N1, dtype=np.float64)
    first = 2.0 * math.pi / N1 * np.outer(k + 0.25, k)
    fwd = np.concatenate([np.cos(first), -np.sin(first)], 0)
    inv = fwd.T / n
    turn = 2.0 * math.pi / n * np.outer(k + 0.25, k)
    tw = np.stack([np.cos(turn), -np.sin(turn)])
    second = 2.0 * math.pi / N1 * np.outer(k, k)
    c, s = np.cos(second), np.sin(second)
    mid = np.block([[c, -s], [s, c]])
    mid_inv = np.block([[c, s], [-s, c]])
    bf = [jnp.asarray(m, F32).astype(BF16) for m in (fwd, mid, mid_inv, inv)]
    return (*bf, jnp.asarray(tw, F32))


def kernel(
    tok_hbm, w_hbm, gk_hbm, gq_hbm, fl_hbm, skip_hbm, fwd_hbm, mid_hbm, midi_hbm, inv_hbm, tw_hbm,
    out_hbm,
    tok, wbuf, wown, gk, gq, fl, skip, fwd, mid, midi, inv, tw,
    z2s, z2r, pa, zs, zr, own, mixed, out,
    fs, fr, xs, xr, ys, yr, bounce, lanes, spec,
    in_sem, w_sem, wown_sem, out_sem,
    z2s_sem, z2r_sem, zs_sem, zr_sem, fs_sem, fr_sem, xs_sem, xr_sem, ys_sem, yr_sem,
):
    s, c = lax.axis_index("seq"), lax.axis_index("chan")
    up, down, far = lax.rem(c + 1, CHAN), lax.rem(c + 3, CHAN), lax.rem(c + 2, CHAN)
    ex, why, core = s // 8, lax.rem(s // 2, 4), lax.rem(s, 2)
    owners = (far, up, down)

    def plane_each(body):
        def step(m, carry):
            q = lax.rem(11 * m, 16)
            chip = lax.rem(ex + q // 4, 4) * 4 + lax.rem(why + lax.rem(q, 4), 4)
            body(chip * 2 + core)
            body(chip * 2 + 1 - core)
            return carry

        lax.fori_loop(1, 16, step, 0)
        body(s + 1 - 2 * core)

    loads = [
        pltpu.make_async_copy(a, b, in_sem.at[i])
        for i, (a, b) in enumerate(
            [(tok_hbm, tok), (gk_hbm, gk), (gq_hbm, gq), (fl_hbm, fl), (skip_hbm, skip), (fwd_hbm, fwd),
             (mid_hbm, mid), (midi_hbm, midi), (inv_hbm, inv), (tw_hbm, tw)]
        )
    ]

    def w_copy(kind, j):
        col = pl.multiple_of(owners[kind] * WIDTH + j * CW, CW)
        slot = lax.rem(j, 2)
        return pltpu.make_async_copy(
            w_hbm.at[:, pl.ds(col, CW)], wbuf.at[kind, slot], w_sem.at[kind, slot]
        )

    def wown_copy(j):
        col = pl.multiple_of(c * WIDTH + j * CW, CW)
        return pltpu.make_async_copy(w_hbm.at[:, pl.ds(col, CW)], wown.at[j], wown_sem.at[j])

    loads[0].start()
    for kind in range(3):
        w_copy(kind, 0).start()
    loads[3].start()
    for kind in range(3):
        w_copy(kind, 1).start()
    for i in (1, 2, 4, 5, 6, 7, 8, 9):
        loads[i].start()
    for j in range(NC):
        wown_copy(j).start()

    barrier = pltpu.get_barrier_semaphore()
    for z in (up, down):
        pl.semaphore_signal(barrier, inc=1, device_id=(s, z), device_id_type=MESH)
    plane_each(
        lambda d: pl.semaphore_signal(barrier, inc=1, device_id=(d, c), device_id_type=MESH)
    )

    loads[0].wait()
    loads[3].wait()

    def z2_copy(j, half):
        rows = pl.ds(half * HALF, HALF)
        return pltpu.make_async_remote_copy(
            z2s.at[j, rows], z2r.at[j, rows], z2s_sem.at[j, half], z2r_sem.at[j, half],
            device_id=(s, (up, down)[half]), device_id_type=MESH,
        )

    def z_copy(j, way):
        return pltpu.make_async_remote_copy(
            zs.at[way, j], zr.at[way, j], zs_sem.at[way, j], zr_sem.at[way, j],
            device_id=(s, (up, down)[way]), device_id_type=MESH,
        )

    def plane_send(src, dst, send_sem, recv_sem, j):
        def one(d):
            pltpu.make_async_remote_copy(
                src.at[j, d], dst.at[j, s], send_sem.at[j], recv_sem.at[j],
                device_id=(d, c), device_id_type=MESH,
            ).start()

        plane_each(one)
        dst[j, s] = src[j, s]

    def plane_wait(src, dst, send_sem, recv_sem, j):
        return pltpu.make_async_remote_copy(
            src.at[j, pl.ds(0, SEQ - 1)], dst.at[j, pl.ds(0, SEQ - 1)],
            send_sem.at[j], recv_sem.at[j], device_id=(s, c), device_id_type=MESH,
        )

    def to_blocks(values, dst, j):
        for a in range(OWN_A):
            part = values[a * N1 : (a + 1) * N1].T.reshape(SEQ, CD, N1)
            bounce[:, a * CD : (a + 1) * CD, :] = part
        dst[j] = bounce[...].astype(BF16)

    def chunk(j):
        return pl.ds(pl.multiple_of(j * CW, CW), CW)

    def finish(j):
        for way in range(2):
            z2_copy(j, way).wait_recv()
            rows = pl.ds(way * HALF, HALF)
            zs[way, j, rows] = (pa[way, j] + z2r[j, rows].astype(F32)).astype(BF16)
            z_copy(j, way).start()

    def project(j, carry):
        for kind in range(3):
            slot = lax.rem(j, 2)
            w_copy(kind, j).wait()
            part = jnp.dot(tok[...], wbuf[kind, slot], preferred_element_type=F32)
            if kind == 0:
                z2s[j] = part.astype(BF16)

                @pl.when(j == 0)
                def _():
                    pl.semaphore_wait(barrier, SEQ + 1)

                z2_copy(j, 0).start()
                z2_copy(j, 1).start()
            else:
                way = kind - 1
                other = 1 - way
                pa[way, j] = part[way * HALF : (way + 1) * HALF]
                zs[way, j, pl.ds(other * HALF, HALF)] = part[
                    other * HALF : (other + 1) * HALF
                ].astype(BF16)

            @pl.when(j + 2 < NC)
            def _():
                w_copy(kind, j + 2).start()

        to_blocks(fl[:, chunk(j)].astype(F32), fs, j)
        plane_send(fs, fr, fs_sem, fr_sem, j)

        @pl.when(j > 0)
        def _():
            finish(j - 1)

        return carry

    lax.fori_loop(0, NC, project, 0)
    finish(NC - 1)

    def project_own(j, carry):
        wown_copy(j).wait()
        own[j] = jnp.dot(tok[...], wown[j], preferred_element_type=F32)
        return carry

    lax.fori_loop(0, NC, project_own, 0)
    for i in (1, 2, 4, 5, 6, 7, 8, 9):
        loads[i].wait()

    def forward(i):
        pair = jnp.concatenate(
            [lanes[pl.ds(i, N1, stride=CD), :], lanes[pl.ds(i + 1, N1, stride=CD), :]], axis=1
        ).astype(BF16)
        first = jnp.dot(fwd[...], pair, preferred_element_type=F32)
        rows = []
        for q in range(2):
            re = first[:N1, q * N1 : (q + 1) * N1]
            im = first[N1:, q * N1 : (q + 1) * N1]
            rows.append(
                jnp.concatenate([re * tw[0] - im * tw[1], re * tw[1] + im * tw[0]], axis=1)
            )
        turned = jnp.concatenate(rows, axis=0).astype(BF16)
        return jnp.dot(turned, mid[...], preferred_element_type=F32)

    def load_lanes(src, j):
        lanes[...] = src[j].astype(F32).reshape(SEQ * BR, N1)

    def transform_filters(j, carry):
        plane_wait(fs, fr, fs_sem, fr_sem, j).wait_recv()
        load_lanes(fr, j)
        for p in range(CD // 2):
            spec[j, p] = forward(2 * p)
        return carry

    lax.fori_loop(0, NC, transform_filters, 0)

    def gather_sums(j):
        z_copy(j, 0).wait_recv()
        z_copy(j, 1).wait_recv()
        value = own[j] + zr[0, j].astype(F32) + zr[1, j].astype(F32)
        mix = (gk[:, chunk(j)].astype(F32) * value).astype(BF16)
        mixed[:, chunk(j)] = mix
        to_blocks(mix.astype(F32), xs, j)
        plane_send(xs, xr, xs_sem, xr_sem, j)

    def convolve(j):
        plane_wait(xs, xr, xs_sem, xr_sem, j).wait_recv()
        load_lanes(xr, j)
        for p in range(CD // 2):
            freq = forward(2 * p)
            filt = spec[j, p]
            re, im = freq[:, :N1], freq[:, N1:]
            fre, fim = filt[:, :N1], filt[:, N1:]
            prod = jnp.concatenate([re * fre - im * fim, re * fim + im * fre], axis=1)
            back = jnp.dot(prod.astype(BF16), midi[...], preferred_element_type=F32)
            tops, bottoms = [], []
            for q in range(2):
                bre = back[q * N1 : (q + 1) * N1, :N1]
                bim = back[q * N1 : (q + 1) * N1, N1:]
                tops.append(bre * tw[0] + bim * tw[1])
                bottoms.append(bim * tw[0] - bre * tw[1])
            turned = jnp.concatenate(
                [jnp.concatenate(tops, axis=1), jnp.concatenate(bottoms, axis=1)], axis=0
            ).astype(BF16)
            conv = jnp.dot(inv[...], turned, preferred_element_type=F32)
            lanes[pl.ds(2 * p, N1, stride=CD), :] = conv[:, :N1]
            lanes[pl.ds(2 * p + 1, N1, stride=CD), :] = conv[:, N1:]
        ys[j] = lanes[...].reshape(SEQ, BR, N1).astype(BF16)
        plane_send(ys, yr, ys_sem, yr_sem, j)

    def out_copy(j):
        return pltpu.make_async_copy(out.at[:, chunk(j)], out_hbm.at[:, chunk(j)], out_sem.at[j])

    def finalize(j):
        plane_wait(ys, yr, ys_sem, yr_sem, j).wait_recv()
        bounce[...] = yr[j].astype(F32)
        for a in range(OWN_A):
            conv = bounce[:, a * CD : (a + 1) * CD, :].reshape(CW, N1).T
            rows = pl.ds(a * N1, N1)
            total = conv + skip[:, chunk(j)] * mixed[rows, chunk(j)].astype(F32)
            out[rows, chunk(j)] = (gq[rows, chunk(j)].astype(F32) * total).astype(BF16)
        out_copy(j).start()

    def pipeline(j, carry):
        @pl.when(j < NC)
        def _():
            gather_sums(j)

        @pl.when(jnp.logical_and(j >= 1, j <= NC))
        def _():
            convolve(j - 1)

        @pl.when(j >= 2)
        def _():
            finalize(j - 2)

        return carry

    lax.fori_loop(0, NC + 2, pipeline, 0)

    def drain(j, carry):
        out_copy(j).wait()
        for way in range(2):
            z2_copy(j, way).wait_send()
            z_copy(j, way).wait_send()
        plane_wait(fs, fr, fs_sem, fr_sem, j).wait_send()
        plane_wait(xs, xr, xs_sem, xr_sem, j).wait_send()
        plane_wait(ys, yr, ys_sem, yr_sem, j).wait_send()
        return carry

    lax.fori_loop(0, NC, drain, 0)


def local(tokens, w_in, gate_k, gate_q, filters, skip):
    any_spec = pl.BlockSpec(memory_space=pl.ANY)
    vm = pltpu.VMEM
    dma = pltpu.SemaphoreType.DMA
    block = (NC, SEQ, BR, N1)
    scratch = [
        vm((ROWS, FEAT), BF16), vm((3, 2, FEAT, CW), BF16), vm((NC, FEAT, CW), BF16),
        vm((ROWS, WIDTH), BF16), vm((ROWS, WIDTH), BF16), vm((ROWS, WIDTH), BF16), vm((1, WIDTH), F32),
        vm((2 * N1, N1), BF16), vm((2 * N1, 2 * N1), BF16), vm((2 * N1, 2 * N1), BF16),
        vm((N1, 2 * N1), BF16), vm((2, N1, N1), F32),
        vm((NC, ROWS, CW), BF16), vm((NC, ROWS, CW), BF16), vm((2, NC, HALF, CW), F32),
        vm((2, NC, ROWS, CW), BF16), vm((2, NC, ROWS, CW), BF16), vm((NC, ROWS, CW), F32),
        vm((ROWS, WIDTH), BF16), vm((ROWS, WIDTH), BF16),
        vm(block, BF16), vm(block, BF16), vm(block, BF16), vm(block, BF16), vm(block, BF16), vm(block, BF16),
        vm((SEQ, BR, N1), F32), vm((SEQ * BR, N1), F32), vm((NC, CD // 2, 2 * N1, 2 * N1), F32),
        dma((10,)), dma((3, 2)), dma((NC,)), dma((NC,)),
        dma((NC, 2)), dma((NC, 2)), dma((2, NC)), dma((2, NC)),
        dma((NC,)), dma((NC,)), dma((NC,)), dma((NC,)), dma((NC,)), dma((NC,)),
    ]
    return pl.pallas_call(
        kernel,
        out_shape=jax.ShapeDtypeStruct((ROWS, WIDTH), BF16),
        in_specs=[any_spec] * 11,
        out_specs=any_spec,
        scratch_shapes=scratch,
        compiler_params=pltpu.CompilerParams(
            collective_id=0, has_side_effects=True, vmem_limit_bytes=60 * 2**20
        ),
        name="hyena_block",
    )(tokens, w_in, gate_k, gate_q, filters, skip.reshape(1, WIDTH), *tables())


def solution(mesh):
    in_specs = (
        P("seq", "chan"),
        P("chan", None),
        P("seq", "chan"),
        P("seq", "chan"),
        P("seq", "chan"),
        P("chan"),
    )
    out_specs = P("seq", "chan")
    return jax.shard_map(local, mesh=mesh, in_specs=in_specs, out_specs=out_specs, check_vma=False)
```

time: 611 us -> 78.1 us (0.13)
  waiting for transfers between devices: 219 us -> 0 us
  blocking collectives: 151 us -> 0 us
  matrix products: 147 us -> 0 us
  Pallas kernels: 0 us -> 75.7 us
  local copies, waits for them, and re-layouts: 48.4 us -> 2.26 us
  other arithmetic: 14.2 us -> 0 us
  between operations: 14.1 us -> 0.01 us
  starting transfers between devices: 13.4 us -> 0 us
    all_to_all x2 -> x0, blocking collectives: 151 us -> none  [the longest x1 119 us: local(): lax.all_to_all(outgoing, 'seq', split_axis=2, concat_axis=1, tiled=True)]
    dot_general x13 -> x0, matrix products: 147 us -> none  [the longest x2 28.2 us: complex_product(): jnp.einsum(form, left_re, right_im, precision=highest)]
    all_to_all x2 -> x0, waiting for transfers between devices: 134 us -> none  [the longest x1 106 us: local(): lax.all_to_all(packed.astype(jnp.bfloat16), 'seq', split_axis=2, concat_a...]
    reduce_scatter x1 -> x0, waiting for transfers between devices: 84.1 us -> none  [local(): value = lax.psum_scatter(terms, 'chan', scatter_dimension=1, tiled=True)]
    pallas_call x0 -> x1, Pallas kernels: none -> 75.7 us  [local(): pl.pallas_call(kernel, out_shape=jax.ShapeDtypeStruct((ROWS, WIDTH), BF16...]
    another operation x6 -> x0, local copies, waits for them, and re-layouts: 35.3 us -> none  [the longest x4 32.1 us: local(): jnp.stack([real, imag], 1)]
    all_to_all x2 -> x0, starting transfers between devices: 13.4 us -> none  [the longest x1 7.79 us: local(): lax.all_to_all(stacked, 'seq', split_axis=1, concat_axis=1, tiled=True)]
    all_to_all x1 -> x0, local copies, waits for them, and re-layouts: 8.53 us -> none  [local(): lax.all_to_all(packed.astype(jnp.bfloat16), 'seq', split_axis=2, concat_a...]
  transfers between devices with their start and end apart: 3 -> 0, of which waited for: 3 -> 0; matrix products, arithmetic and copies ran while one was open for 0% -> 0% of each run, Pallas kernels for 0% -> 0%
where the time goes in v1:
time: 78.1 us; the launch traced here: 78 us
  Pallas kernels  75.7 us (97%)
  local copies, waits for them, and re-layouts  2.26 us (3%)
    pallas_call x1, Pallas kernels, local(): pl.pallas_call(kernel, out_shape=jax.ShapeDtypeStruct((ROWS, WIDTH), BF16...  75.7 us
    unnamed x1, local copies, waits for them, and re-layouts  2.26 us

profile of v1, /device:TPU:1, one launch (start us, length us, event | category | flops | bytes accessed | tf_op | source)
XLA Modules:
  0.0 78.0 jit_solution(16287368711108316786)
XLA Ops:
  0.0 75.7 %hyena_block.1 = bf16[512,1024]{1,0:T(8,128)(2,1)} custom-call(bf16[512,2048]{1,0:T(8,128)(2,1)} %tok_hbm.1, bf16[2048,4096]{1,0:T(8,128)(2,1)} %w_hbm.1, bf16[512,1024]{1,0:T(8,128)(2,1)} %gk_hbm.1, bf16[512,1024]{1,0:T(8,128)(2,1)} %gq_hbm.1, bf16[512,1024]{1,0:T(8,128)(2,1)} %fl_hbm.1, f32[1,1024]{1,0:T(1,128)} %bitcast.1, ...), custom_call_target="tpu_custom_call" | custom-call | tf_op jit(solution)/shard_map/hyena_block/pallas_call | solution.py:323
  75.7 2.3 %copy.13 = bf16[512,1024]{1,0:T(8,128)(2,1)} copy(bf16[512,1024]{1,0:T(8,128)(2,1)} %hyena_block.1) | data formatting | bytes 2097152

commit v2 on v1

--- a/solution.py
+++ b/solution.py
@@ -44,7 +44,7 @@
     tok_hbm, w_hbm, gk_hbm, gq_hbm, fl_hbm, skip_hbm, fwd_hbm, mid_hbm, midi_hbm, inv_hbm, tw_hbm,
     out_hbm,
     tok, wbuf, wown, gk, gq, fl, skip, fwd, mid, midi, inv, tw,
-    z2s, z2r, pa, zs, zr, own, mixed, out,
+    z2s, z2r, zs, zr, own, mixed, out,
     fs, fr, xs, xr, ys, yr, bounce, lanes, spec,
     in_sem, w_sem, wown_sem, out_sem,
     z2s_sem, z2r_sem, zs_sem, zr_sem, fs_sem, fr_sem, xs_sem, xr_sem, ys_sem, yr_sem,
@@ -143,56 +143,53 @@
     def chunk(j):
         return pl.ds(pl.multiple_of(j * CW, CW), CW)
 
-    def finish(j):
+    def project(kind, j):
+        slot = lax.rem(j, 2)
+        w_copy(kind, j).wait()
+        part = jnp.dot(tok[...], wbuf[kind, slot], preferred_element_type=F32)
+
+        @pl.when(j + 2 < NC)
+        def _():
+            w_copy(kind, j + 2).start()
+
+        return part
+
+    def project_far(j, carry):
+        z2s[j] = project(0, j).astype(BF16)
+
+        @pl.when(j == 0)
+        def _():
+            pl.semaphore_wait(barrier, SEQ + 1)
+
+        z2_copy(j, 0).start()
+        z2_copy(j, 1).start()
+        return carry
+
+    def project_near(j, carry):
         for way in range(2):
+            part = project(1 + way, j)
+            mine, other = pl.ds(way * HALF, HALF), pl.ds((1 - way) * HALF, HALF)
             z2_copy(j, way).wait_recv()
-            rows = pl.ds(way * HALF, HALF)
-            zs[way, j, rows] = (pa[way, j] + z2r[j, rows].astype(F32)).astype(BF16)
+            zs[way, j, other] = part[(1 - way) * HALF : (2 - way) * HALF].astype(BF16)
+            zs[way, j, mine] = (
+                part[way * HALF : (way + 1) * HALF] + z2r[j, mine].astype(F32)
+            ).astype(BF16)
             z_copy(j, way).start()
-
-    def project(j, carry):
-        for kind in range(3):
-            slot = lax.rem(j, 2)
-            w_copy(kind, j).wait()
-            part = jnp.dot(tok[...], wbuf[kind, slot], preferred_element_type=F32)
-            if kind == 0:
-                z2s[j] = part.astype(BF16)
-
-                @pl.when(j == 0)
-                def _():
-                    pl.semaphore_wait(barrier, SEQ + 1)
-
-                z2_copy(j, 0).start()
-                z2_copy(j, 1).start()
-            else:
-                way = kind - 1
-                other = 1 - way
-                pa[way, j] = part[way * HALF : (way + 1) * HALF]
-                zs[way, j, pl.ds(other * HALF, HALF)] = part[
-                    other * HALF : (other + 1) * HALF
-                ].astype(BF16)
-
-            @pl.when(j + 2 < NC)
-            def _():
-                w_copy(kind, j + 2).start()
-
-        to_blocks(fl[:, chunk(j)].astype(F32), fs, j)
-        plane_send(fs, fr, fs_sem, fr_sem, j)
-
-        @pl.when(j > 0)
-        def _():
-            finish(j - 1)
-
-        return carry
-
-    lax.fori_loop(0, NC, project, 0)
-    finish(NC - 1)
+        return carry
 
     def project_own(j, carry):
         wown_copy(j).wait()
         own[j] = jnp.dot(tok[...], wown[j], preferred_element_type=F32)
         return carry
 
+    def block_filters(j, carry):
+        to_blocks(fl[:, chunk(j)].astype(F32), fs, (0, slice(None), pl.ds(pl.multiple_of(j * BR, BR), BR)))
+        return carry
+
+    lax.fori_loop(0, NC, project_far, 0)
+    lax.fori_loop(0, NC, block_filters, 0)
+    plane_send(fs, fr, fs_sem, fr_sem, 0)
+    lax.fori_loop(0, NC, project_near, 0)
     lax.fori_loop(0, NC, project_own, 0)
     for i in (1, 2, 4, 5, 6, 7, 8, 9):
         loads[i].wait()
@@ -216,13 +213,13 @@
         lanes[...] = src[j].astype(F32).reshape(SEQ * BR, N1)
 
     def transform_filters(j, carry):
-        plane_wait(fs, fr, fs_sem, fr_sem, j).wait_recv()
-        load_lanes(fr, j)
+        load_lanes(fr, (0, slice(None), pl.ds(pl.multiple_of(j * BR, BR), BR)))
         for p in range(CD // 2):
             spec[j, p] = forward(2 * p)
         return carry
 
-    lax.fori_loop(0, NC, transform_filters, 0)
+    plane_wait(fs, fr, fs_sem, fr_sem, 0).wait_recv()
+    transform_filters(0, 0)
 
     def gather_sums(j):
         z_copy(j, 0).wait_recv()
@@ -272,32 +269,37 @@
         out_copy(j).start()
 
     def pipeline(j, carry):
-        @pl.when(j < NC)
+        gather_sums(j)
+
+        @pl.when(j == 0)
         def _():
-            gather_sums(j)
-
-        @pl.when(jnp.logical_and(j >= 1, j <= NC))
+            lax.fori_loop(1, NC, transform_filters, 0)
+
+        @pl.when(j >= 1)
         def _():
             convolve(j - 1)
 
-        @pl.when(j >= 2)
-        def _():
-            finalize(j - 2)
-
-        return carry
-
-    lax.fori_loop(0, NC + 2, pipeline, 0)
+        return carry
+
+    def finish(j, carry):
+        finalize(j)
+        return carry
+
+    lax.fori_loop(0, NC, pipeline, 0)
+    lax.fori_loop(0, NC - 2, finish, 0)
+    convolve(NC - 1)
+    lax.fori_loop(NC - 2, NC, finish, 0)
 
     def drain(j, carry):
         out_copy(j).wait()
         for way in range(2):
             z2_copy(j, way).wait_send()
             z_copy(j, way).wait_send()
-        plane_wait(fs, fr, fs_sem, fr_sem, j).wait_send()
         plane_wait(xs, xr, xs_sem, xr_sem, j).wait_send()
         plane_wait(ys, yr, ys_sem, yr_sem, j).wait_send()
         return carry
 
+    plane_wait(fs, fr, fs_sem, fr_sem, 0).wait_send()
     lax.fori_loop(0, NC, drain, 0)
 
 
@@ -311,14 +313,15 @@
         vm((ROWS, WIDTH), BF16), vm((ROWS, WIDTH), BF16), vm((ROWS, WIDTH), BF16), vm((1, WIDTH), F32),
         vm((2 * N1, N1), BF16), vm((2 * N1, 2 * N1), BF16), vm((2 * N1, 2 * N1), BF16),
         vm((N1, 2 * N1), BF16), vm((2, N1, N1), F32),
-        vm((NC, ROWS, CW), BF16), vm((NC, ROWS, CW), BF16), vm((2, NC, HALF, CW), F32),
+        vm((NC, ROWS, CW), BF16), vm((NC, ROWS, CW), BF16),
         vm((2, NC, ROWS, CW), BF16), vm((2, NC, ROWS, CW), BF16), vm((NC, ROWS, CW), F32),
         vm((ROWS, WIDTH), BF16), vm((ROWS, WIDTH), BF16),
-        vm(block, BF16), vm(block, BF16), vm(block, BF16), vm(block, BF16), vm(block, BF16), vm(block, BF16),
+        vm((1, SEQ, NC * BR, N1), BF16), vm((1, SEQ, NC * BR, N1), BF16),
+        vm(block, BF16), vm(block, BF16), vm(block, BF16), vm(block, BF16),
         vm((SEQ, BR, N1), F32), vm((SEQ * BR, N1), F32), vm((NC, CD // 2, 2 * N1, 2 * N1), F32),
         dma((10,)), dma((3, 2)), dma((NC,)), dma((NC,)),
         dma((NC, 2)), dma((NC, 2)), dma((2, NC)), dma((2, NC)),
-        dma((NC,)), dma((NC,)), dma((NC,)), dma((NC,)), dma((NC,)), dma((NC,)),
+        dma((1,)), dma((1,)), dma((NC,)), dma((NC,)), dma((NC,)), dma((NC,)),
     ]
     return pl.pallas_call(
         kernel,

time: 78.1 us -> 65.8 us (0.84)
  Pallas kernels: 75.7 us -> 63.3 us
    pallas_call x1, Pallas kernels: 75.7 us -> 63.3 us  [local(): pl.pallas_call(kernel, out_shape=jax.ShapeDtypeStruct((ROWS, WIDTH), BF16...]
where the time goes in v2:
time: 65.8 us; the launch traced here: 65.6 us
  Pallas kernels  63.3 us (96%)
  local copies, waits for them, and re-layouts  2.26 us (3%)
    pallas_call x1, Pallas kernels, local(): pl.pallas_call(kernel, out_shape=jax.ShapeDtypeStruct((ROWS, WIDTH), BF16...  63.3 us
    unnamed x1, local copies, waits for them, and re-layouts  2.26 us

profile of v2, /device:TPU:1, one launch (start us, length us, event | category | flops | bytes accessed | tf_op | source)
XLA Modules:
  0.0 65.6 jit_solution(15239086641390462753)
XLA Ops:
  0.0 63.3 %hyena_block.1 = bf16[512,1024]{1,0:T(8,128)(2,1)} custom-call(bf16[512,2048]{1,0:T(8,128)(2,1)} %tok_hbm.1, bf16[2048,4096]{1,0:T(8,128)(2,1)} %w_hbm.1, bf16[512,1024]{1,0:T(8,128)(2,1)} %gk_hbm.1, bf16[512,1024]{1,0:T(8,128)(2,1)} %gq_hbm.1, bf16[512,1024]{1,0:T(8,128)(2,1)} %fl_hbm.1, f32[1,1024]{1,0:T(1,128)} %bitcast.1, ...), custom_call_target="tpu_custom_call" | custom-call | tf_op jit(solution)/shard_map/hyena_block/pallas_call | solution.py:326
  63.3 2.3 %copy.13 = bf16[512,1024]{1,0:T(8,128)(2,1)} copy(bf16[512,1024]{1,0:T(8,128)(2,1)} %hyena_block.1) | data formatting | bytes 2097152

commit v3 on v2

--- a/solution.py
+++ b/solution.py
@@ -43,16 +43,15 @@
 def kernel(
     tok_hbm, w_hbm, gk_hbm, gq_hbm, fl_hbm, skip_hbm, fwd_hbm, mid_hbm, midi_hbm, inv_hbm, tw_hbm,
     out_hbm,
-    tok, wbuf, wown, gk, gq, fl, skip, fwd, mid, midi, inv, tw,
+    tok, wfar, wnear, wown, gk, gq, fl, skip, fwd, mid, midi, inv, tw,
     z2s, z2r, zs, zr, own, mixed, out,
-    fs, fr, xs, xr, ys, yr, bounce, lanes, spec,
-    in_sem, w_sem, wown_sem, out_sem,
+    fs, fr, xs, xr, ys, yr, bounce, lanes, turns, spec, pos, first, rows, second, back,
+    in_sem, wfar_sem, wnear_sem, wown_sem, out_sem,
     z2s_sem, z2r_sem, zs_sem, zr_sem, fs_sem, fr_sem, xs_sem, xr_sem, ys_sem, yr_sem,
 ):
     s, c = lax.axis_index("seq"), lax.axis_index("chan")
     up, down, far = lax.rem(c + 1, CHAN), lax.rem(c + 3, CHAN), lax.rem(c + 2, CHAN)
     ex, why, core = s // 8, lax.rem(s // 2, 4), lax.rem(s, 2)
-    owners = (far, up, down)
 
     def plane_each(body):
         def step(m, carry):
@@ -73,27 +72,22 @@
         )
     ]
 
-    def w_copy(kind, j):
-        col = pl.multiple_of(owners[kind] * WIDTH + j * CW, CW)
+    def w_copy(owner, j, dst, sem):
+        col = pl.multiple_of(owner * WIDTH + j * CW, CW)
+        return pltpu.make_async_copy(w_hbm.at[:, pl.ds(col, CW)], dst, sem)
+
+    def far_copy(j):
+        return w_copy(far, j, wfar.at[j], wfar_sem.at[j])
+
+    def near_copy(way, j):
         slot = lax.rem(j, 2)
-        return pltpu.make_async_copy(
-            w_hbm.at[:, pl.ds(col, CW)], wbuf.at[kind, slot], w_sem.at[kind, slot]
-        )
-
-    def wown_copy(j):
-        col = pl.multiple_of(c * WIDTH + j * CW, CW)
-        return pltpu.make_async_copy(w_hbm.at[:, pl.ds(col, CW)], wown.at[j], wown_sem.at[j])
+        return w_copy((up, down)[way], j, wnear.at[way, slot], wnear_sem.at[way, slot])
+
+    def own_copy(j):
+        return w_copy(c, j, wown.at[j], wown_sem.at[j])
 
     loads[0].start()
-    for kind in range(3):
-        w_copy(kind, 0).start()
-    loads[3].start()
-    for kind in range(3):
-        w_copy(kind, 1).start()
-    for i in (1, 2, 4, 5, 6, 7, 8, 9):
-        loads[i].start()
-    for j in range(NC):
-        wown_copy(j).start()
+    far_copy(0).start()
 
     barrier = pltpu.get_barrier_semaphore()
     for z in (up, down):
@@ -103,12 +97,14 @@
     )
 
     loads[0].wait()
-    loads[3].wait()
+    far_copy(0).wait()
+    for j in range(1, NC):
+        far_copy(j).start()
 
     def z2_copy(j, half):
-        rows = pl.ds(half * HALF, HALF)
+        half_rows = pl.ds(half * HALF, HALF)
         return pltpu.make_async_remote_copy(
-            z2s.at[j, rows], z2r.at[j, rows], z2s_sem.at[j, half], z2r_sem.at[j, half],
+            z2s.at[j, half_rows], z2r.at[j, half_rows], z2s_sem.at[j, half], z2r_sem.at[j, half],
             device_id=(s, (up, down)[half]), device_id_type=MESH,
         )
 
@@ -143,19 +139,12 @@
     def chunk(j):
         return pl.ds(pl.multiple_of(j * CW, CW), CW)
 
-    def project(kind, j):
-        slot = lax.rem(j, 2)
-        w_copy(kind, j).wait()
-        part = jnp.dot(tok[...], wbuf[kind, slot], preferred_element_type=F32)
-
-        @pl.when(j + 2 < NC)
-        def _():
-            w_copy(kind, j + 2).start()
-
-        return part
-
     def project_far(j, carry):
-        z2s[j] = project(0, j).astype(BF16)
+        @pl.when(j > 0)
+        def _():
+            far_copy(j).wait()
+
+        z2s[j] = jnp.dot(tok[...], wfar[j], preferred_element_type=F32).astype(BF16)
 
         @pl.when(j == 0)
         def _():
@@ -163,11 +152,24 @@
 
         z2_copy(j, 0).start()
         z2_copy(j, 1).start()
+
+        @pl.when(j == 0)
+        def _():
+            loads[3].start()
+            for way in range(2):
+                near_copy(way, 0).start()
+
         return carry
 
     def project_near(j, carry):
         for way in range(2):
-            part = project(1 + way, j)
+            near_copy(way, j).wait()
+            part = jnp.dot(tok[...], wnear[way, lax.rem(j, 2)], preferred_element_type=F32)
+
+            @pl.when(j + 2 < NC)
+            def _():
+                near_copy(way, j + 2).start()
+
             mine, other = pl.ds(way * HALF, HALF), pl.ds((1 - way) * HALF, HALF)
             z2_copy(j, way).wait_recv()
             zs[way, j, other] = part[(1 - way) * HALF : (2 - way) * HALF].astype(BF16)
@@ -178,7 +180,7 @@
         return carry
 
     def project_own(j, carry):
-        wown_copy(j).wait()
+        own_copy(j).wait()
         own[j] = jnp.dot(tok[...], wown[j], preferred_element_type=F32)
         return carry
 
@@ -187,35 +189,41 @@
         return carry
 
     lax.fori_loop(0, NC, project_far, 0)
+    for way in range(2):
+        near_copy(way, 1).start()
+    for i in (1, 4, 5, 6, 9):
+        loads[i].start()
+    loads[3].wait()
     lax.fori_loop(0, NC, block_filters, 0)
     plane_send(fs, fr, fs_sem, fr_sem, 0)
+    for j in range(NC):
+        own_copy(j).start()
+    for i in (2, 7, 8):
+        loads[i].start()
     lax.fori_loop(0, NC, project_near, 0)
     lax.fori_loop(0, NC, project_own, 0)
     for i in (1, 2, 4, 5, 6, 7, 8, 9):
         loads[i].wait()
 
-    def forward(i):
-        pair = jnp.concatenate(
-            [lanes[pl.ds(i, N1, stride=CD), :], lanes[pl.ds(i + 1, N1, stride=CD), :]], axis=1
-        ).astype(BF16)
-        first = jnp.dot(fwd[...], pair, preferred_element_type=F32)
-        rows = []
-        for q in range(2):
-            re = first[:N1, q * N1 : (q + 1) * N1]
-            im = first[N1:, q * N1 : (q + 1) * N1]
-            rows.append(
-                jnp.concatenate([re * tw[0] - im * tw[1], re * tw[1] + im * tw[0]], axis=1)
-            )
-        turned = jnp.concatenate(rows, axis=0).astype(BF16)
-        return jnp.dot(turned, mid[...], preferred_element_type=F32)
+    def column(i):
+        return pl.ds(i * N1, N1)
+
+    def forward():
+        for i in range(CD):
+            pos[:, column(i)] = lanes[pl.ds(i, N1, stride=CD), :].astype(BF16)
+        first[...] = jnp.dot(fwd[...], pos[...], preferred_element_type=F32)
+        for i in range(CD):
+            re, im = first[:N1, column(i)], first[N1:, column(i)]
+            rows[column(i), :N1] = (re * tw[0] - im * tw[1]).astype(BF16)
+            rows[column(i), N1:] = (re * tw[1] + im * tw[0]).astype(BF16)
+        return jnp.dot(rows[...], mid[...], preferred_element_type=F32)
 
     def load_lanes(src, j):
         lanes[...] = src[j].astype(F32).reshape(SEQ * BR, N1)
 
     def transform_filters(j, carry):
         load_lanes(fr, (0, slice(None), pl.ds(pl.multiple_of(j * BR, BR), BR)))
-        for p in range(CD // 2):
-            spec[j, p] = forward(2 * p)
+        spec[j] = forward()
         return carry
 
     plane_wait(fs, fr, fs_sem, fr_sem, 0).wait_recv()
@@ -233,26 +241,21 @@
     def convolve(j):
         plane_wait(xs, xr, xs_sem, xr_sem, j).wait_recv()
         load_lanes(xr, j)
-        for p in range(CD // 2):
-            freq = forward(2 * p)
-            filt = spec[j, p]
-            re, im = freq[:, :N1], freq[:, N1:]
-            fre, fim = filt[:, :N1], filt[:, N1:]
-            prod = jnp.concatenate([re * fre - im * fim, re * fim + im * fre], axis=1)
-            back = jnp.dot(prod.astype(BF16), midi[...], preferred_element_type=F32)
-            tops, bottoms = [], []
-            for q in range(2):
-                bre = back[q * N1 : (q + 1) * N1, :N1]
-                bim = back[q * N1 : (q + 1) * N1, N1:]
-                tops.append(bre * tw[0] + bim * tw[1])
-                bottoms.append(bim * tw[0] - bre * tw[1])
-            turned = jnp.concatenate(
-                [jnp.concatenate(tops, axis=1), jnp.concatenate(bottoms, axis=1)], axis=0
-            ).astype(BF16)
-            conv = jnp.dot(inv[...], turned, preferred_element_type=F32)
-            lanes[pl.ds(2 * p, N1, stride=CD), :] = conv[:, :N1]
-            lanes[pl.ds(2 * p + 1, N1, stride=CD), :] = conv[:, N1:]
-        ys[j] = lanes[...].reshape(SEQ, BR, N1).astype(BF16)
+        second[...] = forward()
+        for i in range(CD):
+            re, im = second[column(i), :N1], second[column(i), N1:]
+            fre, fim = spec[j, column(i), :N1], spec[j, column(i), N1:]
+            rows[column(i), :N1] = (re * fre - im * fim).astype(BF16)
+            rows[column(i), N1:] = (re * fim + im * fre).astype(BF16)
+        second[...] = jnp.dot(rows[...], midi[...], preferred_element_type=F32)
+        for i in range(CD):
+            re, im = second[column(i), :N1], second[column(i), N1:]
+            back[:N1, column(i)] = (re * tw[0] + im * tw[1]).astype(BF16)
+            back[N1:, column(i)] = (im * tw[0] - re * tw[1]).astype(BF16)
+        conv = jnp.dot(inv[...], back[...], preferred_element_type=F32)
+        for i in range(CD):
+            turns[pl.ds(i, N1, stride=CD), :] = conv[:, i * N1 : (i + 1) * N1]
+        ys[j] = turns[...].reshape(SEQ, BR, N1).astype(BF16)
         plane_send(ys, yr, ys_sem, yr_sem, j)
 
     def out_copy(j):
@@ -263,9 +266,9 @@
         bounce[...] = yr[j].astype(F32)
         for a in range(OWN_A):
             conv = bounce[:, a * CD : (a + 1) * CD, :].reshape(CW, N1).T
-            rows = pl.ds(a * N1, N1)
-            total = conv + skip[:, chunk(j)] * mixed[rows, chunk(j)].astype(F32)
-            out[rows, chunk(j)] = (gq[rows, chunk(j)].astype(F32) * total).astype(BF16)
+            own_rows = pl.ds(a * N1, N1)
+            total = conv + skip[:, chunk(j)] * mixed[own_rows, chunk(j)].astype(F32)
+            out[own_rows, chunk(j)] = (gq[own_rows, chunk(j)].astype(F32) * total).astype(BF16)
         out_copy(j).start()
 
     def pipeline(j, carry):
@@ -309,7 +312,7 @@
     dma = pltpu.SemaphoreType.DMA
     block = (NC, SEQ, BR, N1)
     scratch = [
-        vm((ROWS, FEAT), BF16), vm((3, 2, FEAT, CW), BF16), vm((NC, FEAT, CW), BF16),
+        vm((ROWS, FEAT), BF16), vm((NC, FEAT, CW), BF16), vm((2, 2, FEAT, CW), BF16), vm((NC, FEAT, CW), BF16),
         vm((ROWS, WIDTH), BF16), vm((ROWS, WIDTH), BF16), vm((ROWS, WIDTH), BF16), vm((1, WIDTH), F32),
         vm((2 * N1, N1), BF16), vm((2 * N1, 2 * N1), BF16), vm((2 * N1, 2 * N1), BF16),
         vm((N1, 2 * N1), BF16), vm((2, N1, N1), F32),
@@ -318,8 +321,10 @@
         vm((ROWS, WIDTH), BF16), vm((ROWS, WIDTH), BF16),
         vm((1, SEQ, NC * BR, N1), BF16), vm((1, SEQ, NC * BR, N1), BF16),
         vm(block, BF16), vm(block, BF16), vm(block, BF16), vm(block, BF16),
-        vm((SEQ, BR, N1), F32), vm((SEQ * BR, N1), F32), vm((NC, CD // 2, 2 * N1, 2 * N1), F32),
-        dma((10,)), dma((3, 2)), dma((NC,)), dma((NC,)),
+        vm((SEQ, BR, N1), F32), vm((SEQ * BR, N1), F32), vm((SEQ * BR, N1), F32), vm((NC, CD * N1, 2 * N1), F32),
+        vm((N1, CD * N1), BF16), vm((2 * N1, CD * N1), F32), vm((CD * N1, 2 * N1), BF16),
+        vm((CD * N1, 2 * N1), F32), vm((2 * N1, CD * N1), BF16),
+        dma((10,)), dma((NC,)), dma((2, 2)), dma((NC,)), dma((NC,)),
         dma((NC, 2)), dma((NC, 2)), dma((2, NC)), dma((2, NC)),
         dma((1,)), dma((1,)), dma((NC,)), dma((NC,)), dma((NC,)), dma((NC,)),
     ]

time: 65.8 us -> 64.6 us (0.982)
  Pallas kernels: 63.3 us -> 62.2 us
    pallas_call x1, Pallas kernels: 63.3 us -> 62.2 us  [local(): pl.pallas_call(kernel, out_shape=jax.ShapeDtypeStruct((ROWS, WIDTH), BF16...]
where the time goes in v3:
time: 64.6 us; the launch traced here: 64.4 us
  Pallas kernels  62.2 us (96%)
  local copies, waits for them, and re-layouts  2.26 us (3%)
    pallas_call x1, Pallas kernels, local(): pl.pallas_call(kernel, out_shape=jax.ShapeDtypeStruct((ROWS, WIDTH), BF16...  62.2 us
    unnamed x1, local copies, waits for them, and re-layouts  2.26 us

profile of v3, /device:TPU:1, one launch (start us, length us, event | category | flops | bytes accessed | tf_op | source)
XLA Modules:
  0.0 64.4 jit_solution(8041323001230749089)
XLA Ops:
  0.0 62.2 %hyena_block.1 = bf16[512,1024]{1,0:T(8,128)(2,1)} custom-call(bf16[512,2048]{1,0:T(8,128)(2,1)} %tok_hbm.1, bf16[2048,4096]{1,0:T(8,128)(2,1)} %w_hbm.1, bf16[512,1024]{1,0:T(8,128)(2,1)} %gk_hbm.1, bf16[512,1024]{1,0:T(8,128)(2,1)} %gq_hbm.1, bf16[512,1024]{1,0:T(8,128)(2,1)} %fl_hbm.1, f32[1,1024]{1,0:T(1,128)} %bitcast.1, ...), custom_call_target="tpu_custom_call" | custom-call | tf_op jit(solution)/shard_map/hyena_block/pallas_call | solution.py:331
  62.2 2.3 %copy.13 = bf16[512,1024]{1,0:T(8,128)(2,1)} copy(bf16[512,1024]{1,0:T(8,128)(2,1)} %hyena_block.1) | data formatting | bytes 2097152

commit v4 on v3

v4 whole, which is shorter than its diff:
```python
import math

import jax
import jax.numpy as jnp
import numpy as np
from jax import lax
from jax.experimental import pallas as pl
from jax.experimental.pallas import tpu as pltpu
from jax.sharding import PartitionSpec as P

MESH = pl.DeviceIdType.MESH
SEQ = 32
CHAN = 4
ROWS = 512
FEAT = 2048
WIDTH = 1024
N1 = 128
OWN_A = ROWS // N1
CHIPS = SEQ // 2
NC = 4
CW = WIDTH // NC
CD = CW // SEQ
BR = OWN_A * CD
HALF = ROWS // 2
HW = CW // 2
LAST = NC - 1
F32, BF16 = jnp.float32, jnp.bfloat16


def tables():
    n = N1 * N1
    k = np.arange(N1, dtype=np.float64)
    first = 2.0 * math.pi / N1 * np.outer(k + 0.25, k)
    fwd = np.concatenate([np.cos(first), -np.sin(first)], 0)
    inv = fwd.T / n
    turn = 2.0 * math.pi / n * np.outer(k + 0.25, k)
    tw = np.stack([np.cos(turn), -np.sin(turn)])
    second = 2.0 * math.pi / N1 * np.outer(k, k)
    c, s = np.cos(second), np.sin(second)
    mid = np.block([[c, -s], [s, c]])
    mid_inv = np.block([[c, s], [-s, c]])
    bf = [jnp.asarray(m, F32).astype(BF16) for m in (fwd, mid, mid_inv, inv)]
    return (*bf, jnp.asarray(tw, F32))


def kernel(
    tok_hbm, w_hbm, gk_hbm, gq_hbm, fl_hbm, skip_hbm, fwd_hbm, mid_hbm, midi_hbm, inv_hbm, tw_hbm,
    out,
    tok, wfar, wnear, wown, gk, gq, fl, skip, fwd, mid, midi, inv, tw,
    z2s, z2r, zs, zr, own, mixed,
    fs, fr, xs, xr, ys, yr, bounce, lanes, turns, spec, pos, first, rows, second, back,
    line_sem, tok_sem, in_sem, wfar_sem, wnear_sem, wown_sem,
    z2s_sem, z2r_sem, zs_sem, zr_sem, fs_sem, fr_sem, xs_sem, xr_sem, ys_sem, yr_sem,
):
    s, c = lax.axis_index("seq"), lax.axis_index("chan")
    up, down, far = lax.rem(c + 1, CHAN), lax.rem(c + 3, CHAN), lax.rem(c + 2, CHAN)
    ex, why, core = s // 8, lax.rem(s // 2, 4), lax.rem(s, 2)

    me = core * CHIPS + s // 2

    def plane_half(body, h):
        def step(m, carry):
            q = lax.rem(11 * m, CHIPS)
            chip = lax.rem(ex + q // 4, 4) * 4 + lax.rem(why + lax.rem(q, 4), 4)
            body(chip * 2 + h, h * CHIPS + chip)
            return carry

        lax.fori_loop(1, CHIPS, step, 0)

    def plane_each(body):
        def step(m, carry):
            q = lax.rem(11 * m, CHIPS)
            chip = lax.rem(ex + q // 4, 4) * 4 + lax.rem(why + lax.rem(q, 4), 4)
            body(chip * 2 + core, core * CHIPS + chip)
            body(chip * 2 + 1 - core, (1 - core) * CHIPS + chip)
            return carry

        lax.fori_loop(1, CHIPS, step, 0)
        body(s + 1 - 2 * core, (1 - core) * CHIPS + s // 2)

    tok_loads = [
        pltpu.make_async_copy(tok_hbm.at[pl.ds(h * HALF, HALF)], tok.at[pl.ds(h * HALF, HALF)], tok_sem.at[h])
        for h in range(2)
    ]
    loads = [
        pltpu.make_async_copy(a, b, in_sem.at[i])
        for i, (a, b) in enumerate(
            [(gk_hbm, gk), (gq_hbm, gq), (fl_hbm, fl), (skip_hbm, skip), (fwd_hbm, fwd),
             (mid_hbm, mid), (midi_hbm, midi), (inv_hbm, inv), (tw_hbm, tw)]
        )
    ]

    def w_copy(owner, j, dst, sem):
        col = pl.multiple_of(owner * WIDTH + j * CW, CW)
        return pltpu.make_async_copy(w_hbm.at[:, pl.ds(col, CW)], dst, sem)

    def far_copy(j):
        return w_copy(far, j, wfar.at[j], wfar_sem.at[j])

    def near_copy(way, j):
        slot = lax.rem(j, 2)
        return w_copy((up, down)[way], j, wnear.at[way, slot], wnear_sem.at[way, slot])

    def own_copy(j):
        return w_copy(c, j, wown.at[j], wown_sem.at[j])

    tok_loads[0].start()
    far_copy(0).start()

    barrier = pltpu.get_barrier_semaphore()
    line = [lax.rem(ex + k, 4) * 8 + lax.rem(s, 8) for k in range(1, 4)]
    for z in (up, down):
        pl.semaphore_signal(barrier, inc=1, device_id=(s, z), device_id_type=MESH)
    for d in line + [ex * 8 + lax.rem(s + k, 8) for k in range(1, 8)]:
        pl.semaphore_signal(barrier, inc=1, device_id=(d, c), device_id_type=MESH)

    def z2_copy(j, half):
        half_rows = pl.ds(half * HALF, HALF)
        return pltpu.make_async_remote_copy(
            z2s.at[j, half_rows], z2r.at[j, half_rows], z2s_sem.at[j, half], z2r_sem.at[j, half],
            device_id=(s, (up, down)[half]), device_id_type=MESH,
        )

    def z_copy(j, way):
        return pltpu.make_async_remote_copy(
            zs.at[way, j], zr.at[way, j], zs_sem.at[way, j], zr_sem.at[way, j],
            device_id=(s, (up, down)[way]), device_id_type=MESH,
        )

    def z_last(h, way):
        cols = pl.ds(pl.multiple_of(h * HW, HW), HW)
        return pltpu.make_async_remote_copy(
            zs.at[way, LAST, :, cols], zr.at[way, LAST, :, cols],
            zs_sem.at[way, LAST + h], zr_sem.at[way, LAST + h],
            device_id=(s, (up, down)[way]), device_id_type=MESH,
        )

    def block_send(src, dst, send_sem, recv_sem, d):
        pltpu.make_async_remote_copy(
            src, dst, send_sem, recv_sem, device_id=(d, c), device_id_type=MESH
        ).start()

    def send_filters():
        plane_each(
            lambda d, slot: block_send(fs.at[slot], fr.at[s], fs_sem.at[0], fr_sem.at[0], d)
        )
        fr[s] = fs[me]

    def send_mixed(j, h):
        def one(d, slot):
            block_send(xs.at[j, slot], xr.at[j, s], xs_sem.at[j], xr_sem.at[j], d)

        plane_half(one, h)

        @pl.when(core == h)
        def _():
            xr[j, s] = xs[j, me]

        @pl.when(core != h)
        def _():
            one(s + 1 - 2 * core, h * CHIPS + s // 2)

    def send_conv(j):
        plane_each(
            lambda d, slot: block_send(
                ys.at[j, d], yr.at[j, me], ys_sem.at[j], yr_sem.at[j, core], d
            )
        )
        yr[j, me] = ys[j, s]

    def block_wait(buf, send_sem, recv_sem, count):
        part = buf.at[pl.ds(0, count)]
        return pltpu.make_async_remote_copy(
            part, part, send_sem, recv_sem, device_id=(s, c), device_id_type=MESH
        )

    def to_blocks(values, h):
        for a in range(OWN_A):
            part = values[a * N1 : (a + 1) * N1].T.reshape(CHIPS, CD, N1)
            bounce[h, :, a * CD : (a + 1) * CD, :] = part
        return bounce[h].astype(BF16)

    def half(j, h):
        return pl.ds(pl.multiple_of(j * CW + h * HW, HW), HW)

    def by_core(h):
        return pl.ds(h * CHIPS, CHIPS)

    def project_far(j, carry):
        far_copy(j).wait()
        z2s[j] = jnp.dot(tok[...], wfar[j], preferred_element_type=F32).astype(BF16)

        @pl.when(j < LAST)
        def _():
            z2_copy(j, 0).start()
            z2_copy(j, 1).start()

        return carry

    def project_near(j, carry):
        for way in range(2):
            near_copy(way, j).wait()
            part = jnp.dot(tok[...], wnear[way, lax.rem(j, 2)], preferred_element_type=F32)

            @pl.when(j + 2 < NC)
            def _():
                near_copy(way, j + 2).start()

            mine, other = pl.ds(way * HALF, HALF), pl.ds((1 - way) * HALF, HALF)
            z2_copy(j, way).wait_recv()
            zs[way, j, other] = part[(1 - way) * HALF : (2 - way) * HALF].astype(BF16)
            zs[way, j, mine] = (
                part[way * HALF : (way + 1) * HALF] + z2r[j, mine].astype(F32)
            ).astype(BF16)

            @pl.when(j == 0)
            def _():
                z_copy(0, way).start()

        return carry

    def start_sums(copy, j):
        for way in range(2):
            copy(j, way).start()

    def project_own(j, carry):
        own_copy(j).wait()
        own[j] = jnp.dot(tok[...], wown[j], preferred_element_type=F32)
        return carry

    def block_filters(j, carry):
        rows_of = pl.ds(pl.multiple_of(j * BR, BR), BR)
        for h in range(2):
            fs[by_core(h), rows_of] = to_blocks(fl[:, half(j, h)].astype(F32), h)
        return carry

    tok_loads[0].wait()
    far_copy(0).wait()
    tok_loads[1].start()
    for j in range(1, NC):
        far_copy(j).start()
    for h in range(2):
        if h:
            tok_loads[1].wait()
        top = pl.ds(h * HALF, HALF)
        z2s[0, top] = jnp.dot(tok[top], wfar[0], preferred_element_type=F32).astype(BF16)
        if not h:
            pl.semaphore_wait(barrier, 12)
        z2_copy(0, h).start()
        if not h:
            for d in line:
                pl.semaphore_signal(line_sem, inc=1, device_id=(d, c), device_id_type=MESH)
    loads[2].start()
    for way in range(2):
        near_copy(way, 0).start()
    lax.fori_loop(1, 2, project_far, 0)
    for way in range(2):
        near_copy(way, 1).start()
    for i in (0, 3, 4, 5, 8):
        loads[i].start()
    loads[2].wait()
    lax.fori_loop(0, NC, block_filters, 0)
    pl.semaphore_wait(line_sem, 3)
    send_filters()
    for j in range(NC):
        own_copy(j).start()
    for i in (1, 6, 7):
        loads[i].start()
    lax.fori_loop(0, 2, project_near, 0)
    lax.fori_loop(2, 3, project_far, 0)
    lax.fori_loop(0, NC, project_own, 0)
    start_sums(z_copy, 1)
    lax.fori_loop(LAST, NC, project_far, 0)
    for i in (0, 1, 3, 4, 5, 6, 7, 8):
        loads[i].wait()

    def column(i):
        return pl.ds(i * N1, N1)

    def forward():
        for i in range(CD):
            pos[:, column(i)] = lanes[pl.ds(i, N1, stride=CD), :].astype(BF16)
        first[...] = jnp.dot(fwd[...], pos[...], preferred_element_type=F32)
        for i in range(CD):
            re, im = first[:N1, column(i)], first[N1:, column(i)]
            rows[column(i), :N1] = (re * tw[0] - im * tw[1]).astype(BF16)
            rows[column(i), N1:] = (re * tw[1] + im * tw[0]).astype(BF16)
        return jnp.dot(rows[...], mid[...], preferred_element_type=F32)

    def load_lanes(src, j):
        lanes[...] = src[j].astype(F32).reshape(SEQ * BR, N1)

    def transform_filters(j, carry):
        load_lanes(fr, (slice(None), pl.ds(pl.multiple_of(j * BR, BR), BR)))
        spec[j] = forward()
        return carry


    def gather_sums(j, h):
        cols = slice(h * HW, (h + 1) * HW)
        value = own[j, :, cols] + zr[0, j, :, cols].astype(F32) + zr[1, j, :, cols].astype(F32)
        mix = (gk[:, half(j, h)].astype(F32) * value).astype(BF16)
        mixed[:, half(j, h)] = mix
        xs[j, by_core(h)] = to_blocks(mix.astype(F32), h)
        send_mixed(j, h)

    def convolve(j):
        block_wait(xr.at[j], xs_sem.at[j], xr_sem.at[j], SEQ - 1).wait_recv()
        load_lanes(xr, j)
        second[...] = forward()
        for i in range(CD):
            re, im = second[column(i), :N1], second[column(i), N1:]
            fre, fim = spec[j, column(i), :N1], spec[j, column(i), N1:]
            rows[column(i), :N1] = (re * fre - im * fim).astype(BF16)
            rows[column(i), N1:] = (re * fim + im * fre).astype(BF16)
        second[...] = jnp.dot(rows[...], midi[...], preferred_element_type=F32)
        for i in range(CD):
            re, im = second[column(i), :N1], second[column(i), N1:]
            back[:N1, column(i)] = (re * tw[0] + im * tw[1]).astype(BF16)
            back[N1:, column(i)] = (im * tw[0] - re * tw[1]).astype(BF16)
        conv = jnp.dot(inv[...], back[...], preferred_element_type=F32)
        for i in range(CD):
            turns[pl.ds(i, N1, stride=CD), :] = conv[:, i * N1 : (i + 1) * N1]
        ys[j] = turns[...].reshape(SEQ, BR, N1).astype(BF16)
        send_conv(j)

    def finalize(j, h):
        @pl.when(core == h)
        def _():
            block_wait(yr.at[j], ys_sem.at[j], yr_sem.at[j, h], CHIPS - 1).wait_recv()

        @pl.when(core != h)
        def _():
            block_wait(yr.at[j], ys_sem.at[j], yr_sem.at[j, h], CHIPS).wait_recv()

        bounce[h] = yr[j, by_core(h)].astype(F32)
        for a in range(OWN_A):
            conv = bounce[h, :, a * CD : (a + 1) * CD, :].reshape(HW, N1).T
            here = pl.ds(a * N1, N1)
            total = conv + skip[:, half(j, h)] * mixed[here, half(j, h)].astype(F32)
            out[here, half(j, h)] = (gq[here, half(j, h)].astype(F32) * total).astype(BF16)

    def gather_chunk(j):
        z_copy(j, 0).wait_recv()
        z_copy(j, 1).wait_recv()
        gather_sums(j, 0)
        gather_sums(j, 1)

    def finish(j, carry):
        finalize(j, 0)
        finalize(j, 1)
        return carry

    def gather_last(h):
        z_last(h, 0).wait_recv()
        z_last(h, 1).wait_recv()
        gather_sums(LAST, h)

    gather_chunk(0)
    start_sums(z2_copy, LAST)
    lax.fori_loop(2, 3, project_near, 0)
    start_sums(z_copy, 2)
    block_wait(fr, fs_sem.at[0], fr_sem.at[0], SEQ - 1).wait_recv()
    lax.fori_loop(0, NC, transform_filters, 0)
    convolve(0)
    gather_chunk(1)
    lax.fori_loop(3, 4, project_near, 0)
    start_sums(z_last, 0)
    gather_chunk(2)
    start_sums(z_last, 1)
    convolve(1)
    gather_last(0)
    gather_last(1)
    convolve(2)
    lax.fori_loop(0, 2, finish, 0)
    convolve(3)
    lax.fori_loop(2, 4, finish, 0)

    def drain(j, carry):
        for h in range(2):
            z2_copy(j, h).wait_send()

            @pl.when(j < LAST)
            def _():
                z_copy(j, h).wait_send()

        block_wait(xr.at[j], xs_sem.at[j], xr_sem.at[j], SEQ - 1).wait_send()
        block_wait(yr.at[j], ys_sem.at[j], yr_sem.at[j, 0], SEQ - 1).wait_send()
        return carry

    for h in range(2):
        for way in range(2):
            z_last(h, way).wait_send()
    block_wait(fr, fs_sem.at[0], fr_sem.at[0], SEQ - 1).wait_send()
    lax.fori_loop(0, NC, drain, 0)


def local(tokens, w_in, gate_k, gate_q, filters, skip):
    any_spec = pl.BlockSpec(memory_space=pl.ANY)
    vm = pltpu.VMEM
    dma = pltpu.SemaphoreType.DMA
    block = (NC, SEQ, BR, N1)
    scratch = [
        vm((ROWS, FEAT), BF16), vm((NC, FEAT, CW), BF16), vm((2, 2, FEAT, CW), BF16), vm((NC, FEAT, CW), BF16),
        vm((ROWS, WIDTH), BF16), vm((ROWS, WIDTH), BF16), vm((ROWS, WIDTH), BF16), vm((1, WIDTH), F32),
        vm((2 * N1, N1), BF16), vm((2 * N1, 2 * N1), BF16), vm((2 * N1, 2 * N1), BF16),
        vm((N1, 2 * N1), BF16), vm((2, N1, N1), F32),
        vm((NC, ROWS, CW), BF16), vm((NC, ROWS, CW), BF16),
        vm((2, NC, ROWS, CW), BF16), vm((2, NC, ROWS, CW), BF16), vm((NC, ROWS, CW), F32),
        vm((ROWS, WIDTH), BF16),
        vm((SEQ, NC * BR, N1), BF16), vm((SEQ, NC * BR, N1), BF16),
        vm(block, BF16), vm(block, BF16), vm(block, BF16), vm(block, BF16),
        vm((2, CHIPS, BR, N1), F32), vm((SEQ * BR, N1), F32), vm((SEQ * BR, N1), F32), vm((NC, CD * N1, 2 * N1), F32),
        vm((N1, CD * N1), BF16), vm((2 * N1, CD * N1), F32), vm((CD * N1, 2 * N1), BF16),
        vm((CD * N1, 2 * N1), F32), vm((2 * N1, CD * N1), BF16),
        pltpu.SemaphoreType.REGULAR, dma((2,)), dma((9,)), dma((NC,)), dma((2, 2)), dma((NC,)),
        dma((NC, 2)), dma((NC, 2)), dma((2, NC + 1)), dma((2, NC + 1)),
        dma((1,)), dma((1,)), dma((NC,)), dma((NC,)), dma((NC,)), dma((NC, 2)),
    ]
    return pl.pallas_call(
        kernel,
        out_shape=pltpu.VMEM((ROWS, WIDTH), BF16),
        in_specs=[any_spec] * 11,
        out_specs=pl.BlockSpec(memory_space=pltpu.VMEM),
        scratch_shapes=scratch,
        compiler_params=pltpu.CompilerParams(
            collective_id=0, has_side_effects=True, vmem_limit_bytes=56 * 2**20
        ),
        name="hyena_block",
    )(tokens, w_in, gate_k, gate_q, filters, skip.reshape(1, WIDTH), *tables())


def solution(mesh):
    in_specs = (
        P("seq", "chan"),
        P("chan", None),
        P("seq", "chan"),
        P("seq", "chan"),
        P("seq", "chan"),
        P("chan"),
    )
    out_specs = P("seq", "chan")
    return jax.shard_map(local, mesh=mesh, in_specs=in_specs, out_specs=out_specs, check_vma=False)
```

time: 64.6 us -> 60.1 us (0.930)
  Pallas kernels: 62.2 us -> 59 us
  local copies, waits for them, and re-layouts: 2.26 us -> 0.97 us
    pallas_call x1, Pallas kernels: 62.2 us -> 59 us  [local(): pl.pallas_call(kernel, out_shape=pltpu.VMEM((ROWS, WIDTH), BF16), in_spec...]
    unnamed x1, local copies, waits for them, and re-layouts: 2.26 us -> 0.97 us
where the time goes in v4:
time: 60.1 us; the launch traced here: 60 us
  Pallas kernels  59 us (98%)
  local copies, waits for them, and re-layouts  0.97 us (2%)
    pallas_call x1, Pallas kernels, local(): pl.pallas_call(kernel, out_shape=pltpu.VMEM((ROWS, WIDTH), BF16), in_spec...  59 us

profile of v4, /device:TPU:1, one launch (start us, length us, event | category | flops | bytes accessed | tf_op | source)
XLA Modules:
  0.0 60.0 jit_solution(15780150238314764069)
XLA Ops:
  0.0 59.0 %hyena_block.1 = bf16[512,1024]{1,0:T(8,128)(2,1)S(1)} custom-call(bf16[512,2048]{1,0:T(8,128)(2,1)} %tok_hbm.1, bf16[2048,4096]{1,0:T(8,128)(2,1)} %w_hbm.1, bf16[512,1024]{1,0:T(8,128)(2,1)} %gk_hbm.1, bf16[512,1024]{1,0:T(8,128)(2,1)} %gq_hbm.1, bf16[512,1024]{1,0:T(8,128)(2,1)} %fl_hbm.1, f32[1,1024]{1,0:T(1,128)} %bitcast.1, ...), custom_call_target="tpu_custom_call" | custom-call | tf_op jit(solution)/shard_map/hyena_block/pallas_call | solution.py:420
  59.0 1.0 %copy.13 = bf16[512,1024]{1,0:T(8,128)(2,1)} copy(bf16[512,1024]{1,0:T(8,128)(2,1)S(1)} %hyena_block.1) | data formatting | bytes 2097152

commit v5 on v4

--- a/solution.py
+++ b/solution.py
@@ -237,8 +237,8 @@
     tok_loads[0].wait()
     far_copy(0).wait()
     tok_loads[1].start()
-    for j in range(1, NC):
-        far_copy(j).start()
+    far_copy(1).start()
+    loads[2].start()
     for h in range(2):
         if h:
             tok_loads[1].wait()
@@ -250,9 +250,10 @@
         if not h:
             for d in line:
                 pl.semaphore_signal(line_sem, inc=1, device_id=(d, c), device_id_type=MESH)
-    loads[2].start()
     for way in range(2):
         near_copy(way, 0).start()
+    for j in range(2, NC):
+        far_copy(j).start()
     lax.fori_loop(1, 2, project_far, 0)
     for way in range(2):
         near_copy(way, 1).start()

time: 60.1 us -> 59.7 us (level)
  no operation moved by 1% of the time
where the time goes in v5:
time: 59.7 us; the launch traced here: 59.6 us
  Pallas kernels  58.6 us (98%)
  local copies, waits for them, and re-layouts  0.97 us (2%)
    pallas_call x1, Pallas kernels, local(): pl.pallas_call(kernel, out_shape=pltpu.VMEM((ROWS, WIDTH), BF16), in_spec...  58.6 us

profile of v5, /device:TPU:1, one launch (start us, length us, event | category | flops | bytes accessed | tf_op | source)
XLA Modules:
  0.0 59.6 jit_solution(10402410579681603240)
XLA Ops:
  0.0 58.6 %hyena_block.1 = bf16[512,1024]{1,0:T(8,128)(2,1)S(1)} custom-call(bf16[512,2048]{1,0:T(8,128)(2,1)} %tok_hbm.1, bf16[2048,4096]{1,0:T(8,128)(2,1)} %w_hbm.1, bf16[512,1024]{1,0:T(8,128)(2,1)} %gk_hbm.1, bf16[512,1024]{1,0:T(8,128)(2,1)} %gq_hbm.1, bf16[512,1024]{1,0:T(8,128)(2,1)} %fl_hbm.1, f32[1,1024]{1,0:T(1,128)} %bitcast.1, ...), custom_call_target="tpu_custom_call" | custom-call | tf_op jit(solution)/shard_map/hyena_block/pallas_call | solution.py:421
  58.6 1.0 %copy.13 = bf16[512,1024]{1,0:T(8,128)(2,1)} copy(bf16[512,1024]{1,0:T(8,128)(2,1)S(1)} %hyena_block.1) | data formatting | bytes 2097152

commit v6 on v5

--- a/solution.py
+++ b/solution.py
@@ -17,6 +17,9 @@
 N1 = 128
 OWN_A = ROWS // N1
 CHIPS = SEQ // 2
+FAR_FIRST = sorted(
+    [(q // 4, q % 4) for q in range(1, CHIPS)], key=lambda o: -min(o[0], 4 - o[0]) - min(o[1], 4 - o[1])
+)
 NC = 4
 CW = WIDTH // NC
 CD = CW // SEQ
@@ -59,23 +62,17 @@
     me = core * CHIPS + s // 2
 
     def plane_half(body, h):
-        def step(m, carry):
-            q = lax.rem(11 * m, CHIPS)
-            chip = lax.rem(ex + q // 4, 4) * 4 + lax.rem(why + lax.rem(q, 4), 4)
+        for dx, dy in FAR_FIRST:
+            chip = lax.rem(ex + dx, 4) * 4 + lax.rem(why + dy, 4)
             body(chip * 2 + h, h * CHIPS + chip)
-            return carry
-
-        lax.fori_loop(1, CHIPS, step, 0)
+
 
     def plane_each(body):
-        def step(m, carry):
-            q = lax.rem(11 * m, CHIPS)
-            chip = lax.rem(ex + q // 4, 4) * 4 + lax.rem(why + lax.rem(q, 4), 4)
+        for dx, dy in FAR_FIRST:
+            chip = lax.rem(ex + dx, 4) * 4 + lax.rem(why + dy, 4)
             body(chip * 2 + core, core * CHIPS + chip)
             body(chip * 2 + 1 - core, (1 - core) * CHIPS + chip)
-            return carry
-
-        lax.fori_loop(1, CHIPS, step, 0)
+
         body(s + 1 - 2 * core, (1 - core) * CHIPS + s // 2)
 
     tok_loads = [

time: 59.7 us -> 58.7 us (0.983)
  Pallas kernels: 58.6 us -> 57.6 us
    pallas_call x1, Pallas kernels: 58.6 us -> 57.6 us  [local(): pl.pallas_call(kernel, out_shape=pltpu.VMEM((ROWS, WIDTH), BF16), in_spec...]
where the time goes in v6:
time: 58.7 us; the launch traced here: 58.6 us
  Pallas kernels  57.6 us (98%)
  local copies, waits for them, and re-layouts  0.97 us (2%)
    pallas_call x1, Pallas kernels, local(): pl.pallas_call(kernel, out_shape=pltpu.VMEM((ROWS, WIDTH), BF16), in_spec...  57.6 us

profile of v6, /device:TPU:1, one launch (start us, length us, event | category | flops | bytes accessed | tf_op | source)
XLA Modules:
  0.0 58.6 jit_solution(9484922855073801936)
XLA Ops:
  0.0 57.6 %hyena_block.1 = bf16[512,1024]{1,0:T(8,128)(2,1)S(1)} custom-call(bf16[512,2048]{1,0:T(8,128)(2,1)} %tok_hbm.1, bf16[2048,4096]{1,0:T(8,128)(2,1)} %w_hbm.1, bf16[512,1024]{1,0:T(8,128)(2,1)} %gk_hbm.1, bf16[512,1024]{1,0:T(8,128)(2,1)} %gq_hbm.1, bf16[512,1024]{1,0:T(8,128)(2,1)} %fl_hbm.1, f32[1,1024]{1,0:T(1,128)} %bitcast.1, ...), custom_call_target="tpu_custom_call" | custom-call | tf_op jit(solution)/shard_map/hyena_block/pallas_call | solution.py:418
  57.6 1.0 %copy.13 = bf16[512,1024]{1,0:T(8,128)(2,1)} copy(bf16[512,1024]{1,0:T(8,128)(2,1)S(1)} %hyena_block.1) | data formatting | bytes 2097152
